TPU v7x, 512 devices: a whole 4x4x16 slice. The times are simulated.
512 devices in a mesh: dp: 16 (over z), seq: 32 (over x, y, core).
Axes of the slice: x: 4, y: 4, z: 16, core: 2. Of those that a mesh axis runs over, the one named last changes fastest.
Arguments:
- tokens: float32 [16, 4096, 2048], P('dp', 'seq'), may hold values from -10 to 10, as said below
- cotangent: float32 [16, 4096, 2048], P('dp', 'seq'), may hold values from -6 to 6
- short_weights: float32 [3, 8, 2048], replicated, may hold values from 0.2 to 0.6
Outputs:
- grad_tokens: float32 [16, 4096, 2048], P('dp', 'seq')
- grad_weights: float32 [3, 8, 2048], P(None, None, 'seq')
Inputs may be any that keep to these rules, and one draw needn't show every extreme that they name: `tokens`: Real-valued activations of order one.
All inputs are finite; a program needn't handle non-finite values.
Results may differ from a plain program's by a relative error of at most 0.0003.
Values sent between devices are 32-bit elements; how exact they have to be, the bound alone decides.
A program may use at most 64 MiB of HBM per device.

v0:
```python
import jax
import jax.numpy as jnp
from jax import lax
from jax.sharding import Mesh
from jax.sharding import PartitionSpec as P

HEAD = 64
D = 2048
K = 8
SEQ = ("seq_0", "seq_1", "seq_2")


def in_one_piece(arrays, axis, split_dim, concat_dim, along):
    both = jnp.concatenate(arrays, axis=along)
    result, at, done = (
        lax.all_to_all(both, axis, split_axis=split_dim, concat_axis=concat_dim, tiled=True),
        0,
        [],
    )
    for a in arrays:
        done.append(lax.slice_in_dim(result, at, at + a.shape[along], axis=along))
        at += a.shape[along]
    return tuple(done)


def cut_along(shard, dim, size):
    before, after = (shard.shape[:dim], shard.shape[dim + 1 :])
    return jnp.moveaxis(shard.reshape(*before, size, -1, *after), dim, 0)


def joined_along(parts, dim):
    shape = list(parts.shape[1:])
    shape[dim] *= parts.shape[0]
    return jnp.moveaxis(parts, 0, dim).reshape(shape)


def exchange_in_order(parts, axes, sequence):
    shape = [lax.axis_size(a) for a in axes]
    parts = parts.reshape(*shape, *parts.shape[1:])
    for k in sequence:
        parts = lax.all_to_all(parts, axes[k], split_axis=k, concat_axis=k, tiled=True)
    return parts.reshape(-1, *parts.shape[len(axes) :])


def exchange_by_chip(shard, groups, sequence, split_dim, concat_dim):
    size = lax.axis_size(groups[0]) * lax.axis_size(groups[1])
    parts = cut_along(shard, split_dim, size)
    return joined_along(exchange_in_order(parts, groups, sequence), concat_dim)


def from_everyone(shard, axis):
    size = lax.axis_size(axis)
    return lax.all_to_all(
        jnp.broadcast_to(shard[None], (size, *shard.shape)), axis, 0, 0, tiled=True
    )


def over_copies(shard, axis):
    everything = from_everyone(shard, axis)
    return jnp.sum(everything, axis=0)


def attend_back(query, key, value, grad_o):
    scale = HEAD ** (-0.5)
    hi = lax.Precision.HIGHEST
    scores = scale * jnp.einsum("qhe,khe->hqk", query, key, precision=hi)
    top = jnp.max(scores, axis=-1, keepdims=True)
    expo = jnp.exp(scores - top)
    probs = expo / jnp.sum(expo, axis=-1, keepdims=True)
    grad_probs = jnp.einsum("qhe,khe->hqk", grad_o, value, precision=hi)
    delta = jnp.sum(probs * grad_probs, axis=-1, keepdims=True)
    grad_scores = probs * (grad_probs - delta)
    grad_q = scale * jnp.einsum("hqk,khe->qhe", grad_scores, key, precision=hi)
    grad_k = scale * jnp.einsum("hqk,qhe->khe", grad_scores, query, precision=hi)
    grad_v = jnp.einsum("hqk,qhe->khe", probs, grad_o, precision=hi)
    return (grad_q, grad_k, grad_v)


def head_backward(query, key, value, grad_o):
    batch, sums, width = query.shape
    heads_here = width // HEAD

    def one_sequence(parts):
        shaped = [p.reshape(sums, heads_here, HEAD) for p in parts]
        grads = attend_back(shaped[0], shaped[1], shaped[2], shaped[3])
        return tuple((g.reshape(sums, width) for g in grads))

    return jax.vmap(one_sequence)((query, key, value, grad_o))


def per_device(tokens, cotangent, short_weights):
    hi = lax.Precision.HIGHEST
    batch = tokens.shape[0]
    col_tokens, col_grad = in_one_piece((tokens, cotangent), SEQ, 2, 1, 0)
    length = col_tokens.shape[1]
    width = col_tokens.shape[2]
    sums = length // K
    start = lax.axis_index(SEQ) * width
    local_weights = lax.dynamic_slice_in_dim(short_weights, start, width, 2)
    grouped = col_tokens.reshape(batch, sums, K, width)
    summary = jnp.einsum("bjic,mic->mbjc", grouped, local_weights, precision=hi)
    grad_o = jnp.sum(col_grad.reshape(batch, sums, K, width), axis=2)
    grad_q, grad_k, grad_v = head_backward(summary[0], summary[1], summary[2], grad_o)
    grad_summary = jnp.stack([grad_q, grad_k, grad_v])
    grad_cols = jnp.einsum("mbjc,mic->bjic", grad_summary, local_weights, precision=hi).reshape(
        batch, length, width
    )
    grad_tokens = exchange_by_chip(grad_cols, (("seq_0", "seq_1"), "seq_2"), (1, 0), 1, 2)
    partial_value = jnp.einsum("mbjc,bjic->mic", grad_summary, grouped, precision=hi)
    raw = over_copies(partial_value, "dp")
    total_sq = over_copies(jnp.sum(raw * raw), SEQ)
    mean_sq = total_sq / (3 * K * D)
    factor = jnp.minimum(1.0, 1.0 / jnp.sqrt(mean_sq + 1e-06))
    return (grad_tokens, raw * factor)


def solution(mesh):
    finer = Mesh(mesh.devices.reshape(mesh.shape["dp"], 4, 4, 2), ("dp", "seq_0", "seq_1", "seq_2"))
    return jax.shard_map(
        per_device,
        mesh=finer,
        in_specs=(P("dp", SEQ, None), P("dp", SEQ, None), P()),
        out_specs=(P("dp", SEQ, None), P(None, None, SEQ)),
        check_vma=False,
    )
```

profile of v0, /device:TPU:1, one launch (start us, length us, event | category | flops | bytes accessed | tf_op | source)
XLA Modules:
  0.0 132.4 jit_solution(3841400276951879412)
XLA Ops:
  0.7 2.4 %copy.54 = f32[1,128,2048]{1,0,2:T(1,128)S(1)} copy(f32[1,128,2048]{2,1,0:T(8,128)} %param.4) | data formatting | bytes 2097152 | tf_op args[1]
  3.7 3.0 %pad_maximum_fusion = f32[2,128,2048]{1,0,2:T(2,128)} fusion(f32[1,128,2048]{1,0,2:T(1,128)S(1)} %copy.54, f32[1,128,2048]{1,0,2:T(1,128)S(1)} %copy.53), kind=kLoop, calls=%fused_computation | loop fusion | flops 524288 | bytes 4194304 | tf_op jit(solution)/shard_map/concatenate | solution.py:14
  6.7 10.5 %all-to-all-start = ((f32[2,128,2048]{1,0,2:T(2,128)}), f32[2,128,2048]{1,0,2:T(2,128)S(1)}, u32[]{:S(2)}, u32[]{:S(2)}) async-start(f32[2,128,2048]{1,0,2:T(2,128)} %pad_maximum_fusion), calls=%async_computation | async-start | bytes 4194304 | tf_op jit(solution)/shard_map/all_to_all | solution.py:16
  17.5 28.2 %all-to-all-done = f32[2,128,2048]{1,0,2:T(2,128)S(1)} async-done(((f32[2,128,2048]{1,0,2:T(2,128)}), f32[2,128,2048]{1,0,2:T(2,128)S(1)}, u32[]{:S(2)}, u32[]{:S(2)}) %all-to-all-start) | async-done | bytes 2097184 | tf_op jit(solution)/shard_map/all_to_all | solution.py:16
  46.9 1.8 %copy.58 = f32[1,32,128,64]{3,2,1,0:T(8,128)S(1)} copy(f32[1,32,128,64]{2,3,1,0:T(8,128)} %get-tuple-element.11) | data formatting | bytes 2097152 | tf_op jit(solution)/shard_map/slice | solution.py:21
  48.8 2.0 %copy.56 = f32[1,32,128,64]{3,2,1,0:T(8,128)} copy(f32[1,32,128,64]{2,3,1,0:T(8,128)S(1)} %get-tuple-element.10) | data formatting | bytes 2097152 | tf_op jit(solution)/shard_map/slice | solution.py:21
  50.7 2.6 %copy.57 = f32[512,8,64]{0,1,2:T(8,128)S(1)} copy(f32[512,8,64]{2,1,0:T(8,128)} %bitcast.67) | data formatting | bytes 2097152 | tf_op jit(solution)/shard_map/reshape.2
  55.3 1.3 %reduce_sum.55 = f32[512,64]{1,0:T(8,128)} reduce(f32[512,8,64]{2,1,0:T(8,128)S(1)} %bitcast.66, f32[]{:T(128)} %constant.12.clone.1), dimensions={1}, to_apply=%region_2.0 | reduce | flops 229376 | bytes 1179652 | tf_op jit(solution)/shard_map/reduce_sum | solution.py:102
  56.7 2.1 %fusion.22 = (f32[512]{0:T(512)S(1)}, f32[512,512]{0,1:T(8,128)S(1)}) fusion(f32[1,1,512,64]{2,0,3,1:T(1,128)} %get-tuple-element.14, f32[1,1,512,64]{2,0,3,1:T(1,128)} %get-tuple-element.13), kind=kOutput, calls=%fused_computation.34 | convolution fusion | flops 201850368 | bytes 1312768 | tf_op jit(solution)/shard_map/vmap(qhe,khe->hqk)/dot_general | solution.py:66
  58.9 1.2 convolution_bitcast_fusion.2
  60.2 1.2 multiply_reduce_fusion
  61.4 1.3 fusion
  63.6 2.2 %convolution_bitcast_fusion.3 = f32[3,8,64]{1,0,2:T(4,128)S(1)} fusion(f32[512,8,64]{0,1,2:T(8,128)S(1)} %copy.57, f32[3,512,64]{1,2,0:T(8,128)S(1)} %maximum_bitcast_fusion), kind=kOutput, calls=%fused_computation.9 | convolution fusion | flops 9437184 | bytes 1447936 | tf_op jit(solution)/shard_map/mbjc,bjic->mic/dot_general | solution.py:109
  66.7 12.9 %all-to-all-start.3 = ((f32[16,1,1536]{2,1,0:T(1,128)}), f32[16,1,1536]{2,1,0:T(1,128)S(1)}, u32[]{:S(2)}, u32[]{:S(2)}) async-start(f32[16,1,1536]{2,1,0:T(1,128)} %reshape.115), calls=%async_computation.3 | async-start | bytes 196608 | tf_op jit(solution)/shard_map/all_to_all | solution.py:53
  79.7 1.4 %convolution_bitcast_fusion = f32[1,512,8,64]{1,2,3,0:T(8,128)S(1)} fusion(f32[3,8,64]{1,0,2:T(4,128)S(1)} %copy.72, f32[3,512,64]{1,2,0:T(8,128)S(1)} %maximum_bitcast_fusion), kind=kOutput, calls=%fused_computation.1 | convolution fusion | flops 9437184 | bytes 1447936 | tf_op jit(solution)/shard_map/mbjc,mic->bjic/dot_general | solution.py:105
  82.2 1.6 %copy.61 = f32[16,2,1,128,64]{3,4,2,0,1:T(8,128)} copy(f32[16,2,1,128,64]{4,3,1,0,2:T(8,128)S(1)} %bitcast.68) | data formatting | bytes 2097152 | tf_op jit(solution)/shard_map/reshape;transpose;reshape;reshape | solution.py:39
  83.7 7.7 %all-to-all-done.3 = f32[16,1,1536]{2,1,0:T(1,128)S(1)} async-done(((f32[16,1,1536]{2,1,0:T(1,128)}), f32[16,1,1536]{2,1,0:T(1,128)S(1)}, u32[]{:S(2)}, u32[]{:S(2)}) %all-to-all-start.3) | async-done | bytes 98336 | tf_op jit(solution)/shard_map/all_to_all | solution.py:53
  91.5 6.4 %all-to-all-start.1 = ((f32[16,2,1,128,64]{3,4,2,0,1:T(8,128)}), f32[16,2,1,128,64]{3,4,2,0,1:T(8,128)S(1)}, u32[]{:S(2)}, u32[]{:S(2)}) async-start(f32[16,2,1,128,64]{3,4,2,0,1:T(8,128)} %copy.61), calls=%async_computation.1 | async-start | bytes 2097152 | tf_op jit(solution)/shard_map/all_to_all | solution.py:41
  100.0 1.2 broadcast_in_dim.5
  101.2 3.5 %all-to-all-start.4 = ((f32[32,1,1]{2,1,0:T(1,128)}), f32[32,1,1]{2,1,0:T(1,128)S(1)}, u32[]{:S(2)}, u32[]{:S(2)}) async-start(f32[32,1,1]{2,1,0:T(1,128)} %broadcast_in_dim.5), calls=%async_computation.4 | async-start | bytes 32768 | tf_op jit(solution)/shard_map/all_to_all | solution.py:53
  105.8 6.0 %all-to-all-done.4 = f32[32,1,1]{2,1,0:T(1,128)S(1)} async-done(((f32[32,1,1]{2,1,0:T(1,128)}), f32[32,1,1]{2,1,0:T(1,128)S(1)}, u32[]{:S(2)}, u32[]{:S(2)}) %all-to-all-start.4) | async-done | bytes 160 | tf_op jit(solution)/shard_map/all_to_all | solution.py:53
  111.8 3.7 %all-to-all-start.2 = ((f32[16,2,1,128,64]{3,4,2,1,0:T(8,128)}), f32[16,2,1,128,64]{3,4,2,1,0:T(8,128)S(1)}, u32[]{:S(2)}, u32[]{:S(2)}) async-start(f32[16,2,1,128,64]{3,4,2,1,0:T(8,128)} %copy.62), calls=%async_computation.2 | async-start | bytes 2097152 | tf_op jit(solution)/shard_map/all_to_all | solution.py:41
  117.4 13.7 %all-to-all-done.2 = f32[16,2,1,128,64]{3,4,2,1,0:T(8,128)S(1)} async-done(((f32[16,2,1,128,64]{3,4,2,1,0:T(8,128)}), f32[16,2,1,128,64]{3,4,2,1,0:T(8,128)S(1)}, u32[]{:S(2)}, u32[]{:S(2)}) %all-to-all-start.2) | async-done | bytes 1048608 | tf_op jit(solution)/shard_map/all_to_all | solution.py:41
  131.1 1.3 copy.67
  (35 shorter events, 11.8 us)
Async XLA Ops:
  0.6 16.6 %copy-start = (f32[3,8,2048]{2,1,0:T(8,128)S(1)}, f32[3,8,2048]{2,1,0:T(8,128)}, u32[]{:S(2)}) copy-start(f32[3,8,2048]{2,1,0:T(8,128)} %param.5) | copy-start | bytes 589828
  0.6 2.5 %copy-start.1 = (f32[1,128,2048]{2,1,0:T(8,128)S(1)}, f32[1,128,2048]{2,1,0:T(8,128)}, u32[]{:S(2)}) copy-start(f32[1,128,2048]{2,1,0:T(8,128)} %param.3) | copy-start | bytes 3145732
  6.7 38.9 %all-to-all-start = ((f32[2,128,2048]{1,0,2:T(2,128)}), f32[2,128,2048]{1,0,2:T(2,128)S(1)}, u32[]{:S(2)}, u32[]{:S(2)}) async-start(f32[2,128,2048]{1,0,2:T(2,128)} %pad_maximum_fusion), calls=%async_computation | async-start | bytes 4194304 | tf_op jit(solution)/shard_map/all_to_all | solution.py:16
  56.7 2.3 %copy-start.4 = (f32[512,64]{1,0:T(8,128)S(1)}, f32[512,64]{1,0:T(8,128)}, u32[]{:S(2)}) copy-start(f32[512,64]{1,0:T(8,128)} %reduce_sum.55) | copy-start | bytes 393220
  58.9 1.2 copy-start.5
  60.2 1.2 copy-start.3
  61.3 1.3 copy-start.2
  66.7 24.7 %all-to-all-start.3 = ((f32[16,1,1536]{2,1,0:T(1,128)}), f32[16,1,1536]{2,1,0:T(1,128)S(1)}, u32[]{:S(2)}, u32[]{:S(2)}) async-start(f32[16,1,1536]{2,1,0:T(1,128)} %reshape.115), calls=%async_computation.3 | async-start | bytes 196608 | tf_op jit(solution)/shard_map/all_to_all | solution.py:53
  91.5 8.5 %all-to-all-start.1 = ((f32[16,2,1,128,64]{3,4,2,0,1:T(8,128)}), f32[16,2,1,128,64]{3,4,2,0,1:T(8,128)S(1)}, u32[]{:S(2)}, u32[]{:S(2)}) async-start(f32[16,2,1,128,64]{3,4,2,0,1:T(8,128)} %copy.61), calls=%async_computation.1 | async-start | bytes 2097152 | tf_op jit(solution)/shard_map/all_to_all | solution.py:41
  101.2 10.6 %all-to-all-start.4 = ((f32[32,1,1]{2,1,0:T(1,128)}), f32[32,1,1]{2,1,0:T(1,128)S(1)}, u32[]{:S(2)}, u32[]{:S(2)}) async-start(f32[32,1,1]{2,1,0:T(1,128)} %broadcast_in_dim.5), calls=%async_computation.4 | async-start | bytes 32768 | tf_op jit(solution)/shard_map/all_to_all | solution.py:53
  111.8 19.3 %all-to-all-start.2 = ((f32[16,2,1,128,64]{3,4,2,1,0:T(8,128)}), f32[16,2,1,128,64]{3,4,2,1,0:T(8,128)S(1)}, u32[]{:S(2)}, u32[]{:S(2)}) async-start(f32[16,2,1,128,64]{3,4,2,1,0:T(8,128)} %copy.62), calls=%async_computation.2 | async-start | bytes 2097152 | tf_op jit(solution)/shard_map/all_to_all | solution.py:41
where the time goes:
time: 134 us; the launch traced here: 132 us
  waiting for transfers between devices  55.6 us (41%)
  starting transfers between devices  37 us (28%)
  local copies, waits for them, and re-layouts  19.7 us (15%)
  matrix products  11.3 us (8%)
  other arithmetic  7.27 us (5%)
  between operations  1.56 us (1%)
    all_to_all x1, waiting for transfers between devices, in_one_piece(): lax.all_to_all(both, axis, split_axis=split_dim, concat_axis=concat_dim,...  28.2 us
    all_to_all x2, starting transfers between devices, from_everyone(): lax.all_to_all(jnp.broadcast_to(shard[None], (size, *shard.shape)), axis,...  16.4 us
    all_to_all x2, waiting for transfers between devices, from_everyone(): lax.all_to_all(jnp.broadcast_to(shard[None], (size, *shard.shape)), axis,...  13.7 us
    all_to_all x2, waiting for transfers between devices, exchange_in_order(): lax.all_to_all(parts, axes[k], split_axis=k, concat_axis=k, tiled=True)  13.7 us
    all_to_all x1, starting transfers between devices, in_one_piece(): lax.all_to_all(both, axis, split_axis=split_dim, concat_axis=concat_dim,...  10.5 us
    all_to_all x2, starting transfers between devices, exchange_in_order(): lax.all_to_all(parts, axes[k], split_axis=k, concat_axis=k, tiled=True)  10 us
    unnamed x18, local copies, waits for them, and re-layouts  5.39 us
    slice x3, local copies, waits for them, and re-layouts, in_one_piece(): done.append(lax.slice_in_dim(result, at, at + a.shape[along], axis=along))  4.96 us
  transfers between devices with their start and end apart: 5, of which 4 were waited for; matrix products, arithmetic and copies ran while one was open for 7% of the time, Pallas kernels for 0%

commit v1 on v0

v1 whole, which is shorter than its diff:
```python
import functools

import jax
import jax.numpy as jnp
from jax import lax
from jax.experimental import pallas as pl
from jax.experimental.pallas import tpu as pltpu
from jax.sharding import PartitionSpec as P

HEAD = 64
LANES = 128
K = 8
GROUP = 16
SCALE = HEAD ** (-0.5)
LOG2E = 1.4426950408889634
MESH = pl.DeviceIdType.MESH
NT = (((1,), (1,)), ((), ()))
NN = (((1,), (0,)), ((), ()))
F32, BF16 = jnp.float32, jnp.bfloat16


def low_half(shape):
    return lax.broadcasted_iota(jnp.int32, shape, len(shape) - 1) < HEAD


def swap_halves(x):
    return pltpu.roll(x, HEAD, len(x.shape) - 1)


def pair_up(x, y):
    low = low_half(x.shape)
    r = swap_halves(jnp.where(low, y, x))
    return jnp.where(low, x, r), jnp.where(low, r, y)


def both_halves(x):
    low = low_half(x.shape)
    r = swap_halves(x)
    return jnp.where(low, x, r), jnp.where(low, r, x)


def dot(a, b, dims):
    return lax.dot_general(a, b, dims, preferred_element_type=F32)


def two_parts(x):
    high = x.astype(BF16).astype(F32)
    return high, x - high


def main_kernel(
    n_seq, n_dp,
    tok_hbm, cot_hbm, w_hbm,
    out_ref, total_ref, squares_ref,
    tok, cot, w, wb,
    send, recv,
    qs, ks, qc, os, vs, oc, kc, kt,
    acc_k, acc_v, acc_q,
    ret, back, rows, dp_all,
    load_sem, send_sem, in_sem, recv_sem,
):
    me = lax.axis_index("seq")
    plane = lax.axis_index("dp")
    tiles = n_seq // 2
    chip, core = me // 2, lax.rem(me, 2)
    cx, cy = chip // 4, lax.rem(chip, 4)
    sums = n_seq * GROUP
    half = sums // 2

    barrier = pltpu.get_barrier_semaphore()

    def hello_seq(d, _):
        other = lax.rem(me + d, n_seq)
        pl.semaphore_signal(barrier, inc=1, device_id=(plane, other), device_id_type=MESH)
        return 0

    def hello_dp(d, _):
        other = lax.rem(plane + d, n_dp)
        pl.semaphore_signal(barrier, inc=1, device_id=(other, me), device_id_type=MESH)
        return 0

    lax.fori_loop(1, n_seq, hello_seq, 0)
    lax.fori_loop(1, n_dp, hello_dp, 0)

    def tile_loads(t):
        lanes = pl.ds(pl.multiple_of(t * LANES, LANES), LANES)
        return (
            pltpu.make_async_copy(tok_hbm.at[0, :, lanes], tok.at[t], load_sem.at[2 * t]),
            pltpu.make_async_copy(cot_hbm.at[0, :, lanes], cot.at[t], load_sem.at[2 * t + 1]),
        )

    def start_loads(t, _):
        for c in tile_loads(t):
            c.start()
        return 0

    lax.fori_loop(0, tiles, start_loads, 0)
    w_load = pltpu.make_async_copy(w_hbm, w, load_sem.at[2 * tiles])
    w_load.start()

    def pack(t, _):
        for c in tile_loads(t):
            c.wait()
        o = None
        for i in range(K):
            x = tok[t, pl.ds(i, GROUP, stride=K), :]
            c = cot[t, pl.ds(i, GROUP, stride=K), :]
            o = c if o is None else o + c
            even, odd = pair_up(x[:8], x[8:])
            send[2 * t, 8 * i : 8 * i + 8] = even
            send[2 * t + 1, 8 * i : 8 * i + 8] = odd
        even, odd = pair_up(o[:8], o[8:])
        send[2 * t, 8 * K : 8 * K + 8] = even
        send[2 * t + 1, 8 * K : 8 * K + 8] = odd
        return 0

    lax.fori_loop(0, tiles, pack, 0)

    w_load.wait()
    lanes = pl.ds(pl.multiple_of(chip * LANES, LANES), LANES)
    for m in range(3):
        first, second = both_halves(w[m, :, lanes])
        mine = jnp.where(core == 0, first, second)
        for i in range(K):
            wb[K * m + i] = jnp.broadcast_to(mine[i : i + 1], (8, LANES))

    pl.semaphore_wait(barrier, n_seq + n_dp - 2)

    def to_seq(src_of, dst, s, sem_of):
        def one(e, _):
            k = e // 2
            x, y = lax.rem(cx + k // 4, 4), lax.rem(cy + lax.rem(k, 4), 4)
            other = (x * 4 + y) * 2 + lax.rem(core + lax.rem(e, 2), 2)
            pltpu.make_async_remote_copy(
                src_ref=src_of(other),
                dst_ref=dst.at[me],
                send_sem=send_sem.at[s],
                recv_sem=sem_of(k),
                device_id=(plane, other),
                device_id_type=MESH,
            ).start()
            return 0

        lax.fori_loop(1, n_seq, one, 0)

    def arrived(dst, sem):
        pltpu.make_async_copy(dst, dst, sem).wait()

    to_seq(lambda h: send.at[h], recv, 0, lambda k: in_sem.at[k])
    pltpu.make_async_copy(send.at[me], recv.at[me], in_sem.at[0]).start()

    def query_role(x, side, cols, r0):
        for part, r in zip(both_halves(x), (r0, half + r0)):
            h, l = two_parts(part)
            at = pl.ds(pl.multiple_of(r, GROUP), GROUP)
            side[at, :LANES] = h.astype(BF16)
            side[at, LANES:] = l.astype(BF16)
            cols[at, :] = jnp.where(low_half(h.shape), h, l).astype(BF16)

    def key_role(x, side, r0, keep=None):
        for part, r in zip(both_halves(x), (r0, half + r0)):
            h, l = two_parts(part)
            at = pl.ds(pl.multiple_of(r, GROUP), GROUP)
            c = jnp.where(low_half(h.shape), h, l)
            side[at, :LANES] = c.astype(BF16)
            side[at, LANES:] = c.astype(BF16)
            if keep is not None:
                keep[at, :] = c

    def take(k, _):
        x, y = lax.rem(cx + 4 - k // 4, 4), lax.rem(cy + 4 - lax.rem(k, 4), 4)
        c = x * 4 + y
        block = recv.at[pl.ds(2 * c, 2)]
        arrived(block, in_sem.at[k])
        pooled = []
        for m in range(3):
            s = None
            for i in range(K):
                a = recv[pl.ds(2 * c, 2), 8 * i : 8 * i + 8, :] * wb[K * m + i]
                s = a if s is None else s + a
            pooled.append(s.reshape(GROUP, LANES))
        o = recv[pl.ds(2 * c, 2), 8 * K : 8 * K + 8, :].reshape(GROUP, LANES)
        r0 = c * GROUP
        query_role(pooled[0], qs, qc, r0)
        key_role(pooled[1], ks, r0, kc)
        key_role(pooled[2], vs, r0)
        query_role(o, os, oc, r0)
        return 0

    lax.fori_loop(0, tiles, take, 0)

    kt[...] = kc[...].T.astype(BF16)
    for b in range(2):
        cols = slice(b * half, (b + 1) * half)
        s = dot(ks[...], qs[cols, :], NT)
        top = jnp.max(s, axis=0, keepdims=True)
        e = jnp.exp2((s - top) * (SCALE * LOG2E))
        p = e * (1.0 / jnp.sum(e, axis=0, keepdims=True))
        gp = dot(vs[...], os[cols, :], NT)
        delta = jnp.sum(p * gp, axis=0, keepdims=True)
        gs = p * (gp - delta)
        p_high, p_low = (x.astype(BF16) for x in two_parts(p))
        g_high, g_low = (x.astype(BF16) for x in two_parts(gs))
        gv = dot(p_high, oc[cols, :], NN) + dot(p_low, oc[cols, :], NN)
        gk = dot(g_high, qc[cols, :], NN) + dot(g_low, qc[cols, :], NN)
        if b == 0:
            acc_v[...] = gv
            acc_k[...] = gk
        else:
            acc_v[...] += gv
            acc_k[...] += gk
        gq = dot(kt[...], g_high, NN) + dot(kt[...], g_low, NN)
        acc_q[b * HEAD : (b + 1) * HEAD, :] = gq[:HEAD] + gq[HEAD:]

    def packed(acc):
        x = acc[...]
        x = x + swap_halves(x)
        return jnp.where(low_half((half, LANES)), x[:half], x[half:]).reshape(n_seq, 8, LANES)

    ret[:, 16:24, :] = packed(acc_v)
    ret[:, 8:16, :] = packed(acc_k) * SCALE
    ret[:, 0:8, :] = (acc_q[...].T * SCALE).reshape(n_seq, 8, LANES)

    def raw_step(s, acc):
        g = [ret[s, 8 * m : 8 * m + 8, :] for m in range(3)]
        done = []
        for i in range(K):
            x = recv[s, 8 * i : 8 * i + 8, :]
            for m in range(3):
                done.append(acc[3 * i + m] + x * g[m])
        return tuple(done)

    zero = jnp.zeros((8, LANES), F32)
    acc = lax.fori_loop(0, n_seq, raw_step, (zero,) * (3 * K))
    for i in range(K):
        for m in range(3):
            r = K * m + i
            rows[r : r + 1, :] = jnp.sum(acc[3 * i + m], axis=0, keepdims=True)
    x = rows[...]
    x = x + swap_halves(x)
    low = low_half((8, LANES))
    dp_all[plane, 0:8] = jnp.where(low, x[0:8], x[8:16])
    dp_all[plane, 8:12] = jnp.where(low[:4], x[16:20], x[20:24])

    for k in range(1, n_dp):
        d = n_dp // 2 + (k // 2 if k % 2 else -(k // 2))
        other = lax.rem(plane + d, n_dp)
        pltpu.make_async_remote_copy(
            src_ref=dp_all.at[plane],
            dst_ref=dp_all.at[plane],
            send_sem=send_sem.at[2],
            recv_sem=recv_sem.at[2],
            device_id=(other, me),
            device_id_type=MESH,
        ).start()

    to_seq(lambda h: ret.at[h], back, 1, lambda k: recv_sem.at[1])
    pltpu.make_async_copy(ret.at[me], back.at[me], recv_sem.at[1]).start()

    others = dp_all.at[pl.ds(0, n_dp - 1)]
    pltpu.make_async_copy(others, others, recv_sem.at[2]).wait()
    total = jnp.sum(dp_all[...], axis=0)
    total_ref[...] = total
    squares_ref[me] = jnp.sum(total * total, axis=0, keepdims=True)
    to_seq(lambda h: squares_ref.at[me], squares_ref, 3, lambda k: recv_sem.at[3])

    arrived(back, recv_sem.at[1])

    def spread(t, _):
        lanes = pl.ds(pl.multiple_of(t * LANES, LANES), LANES)
        g = []
        for m in range(3):
            at = slice(8 * m, 8 * m + 8)
            g.append(jnp.concatenate(pair_up(back[2 * t, at], back[2 * t + 1, at]), axis=0))
        ws = [w[m, :, lanes] for m in range(3)]
        for j in range(GROUP):
            out_ref[0, 8 * j : 8 * j + 8, lanes] = (
                ws[0] * g[0][j : j + 1] + ws[1] * g[1][j : j + 1] + ws[2] * g[2][j : j + 1]
            )
        return 0

    lax.fori_loop(0, tiles, spread, 0)

    rest = squares_ref.at[pl.ds(0, n_seq - 1)]
    arrived(rest, recv_sem.at[3])
    for s, src in enumerate((send, ret, None, squares_ref)):
        src = others if src is None else src.at[pl.ds(0, n_seq - 1)]
        pltpu.make_async_copy(src, src, send_sem.at[s]).wait()


def main_call(tokens, cotangent, short_weights, n_seq, n_dp):
    tiles, sums = n_seq // 2, n_seq * GROUP
    vmem = pl.BlockSpec(memory_space=pltpu.VMEM)
    hbm = pl.BlockSpec(memory_space=pltpu.HBM)

    def v(*shape, dtype=F32):
        return pltpu.VMEM(shape, dtype)

    return pl.pallas_call(
        functools.partial(main_kernel, n_seq, n_dp),
        out_shape=(
            jax.ShapeDtypeStruct((1, GROUP * K, tiles * LANES), F32),
            jax.ShapeDtypeStruct((12, LANES), F32),
            jax.ShapeDtypeStruct((n_seq, 1, LANES), F32),
        ),
        in_specs=[hbm] * 3,
        out_specs=(vmem,) * 3,
        scratch_shapes=[
            v(tiles, GROUP * K, LANES), v(tiles, GROUP * K, LANES), v(3, K, tiles * LANES), v(3 * K, 8, LANES),
            v(n_seq, 8 * K + 8, LANES), v(n_seq, 8 * K + 8, LANES),
            v(sums, 256, dtype=BF16), v(sums, 256, dtype=BF16), v(sums, LANES, dtype=BF16),
            v(sums, 256, dtype=BF16), v(sums, 256, dtype=BF16), v(sums, LANES, dtype=BF16),
            v(sums, LANES), v(LANES, sums, dtype=BF16),
            v(sums, LANES), v(sums, LANES), v(LANES, sums // 2),
            v(n_seq, 24, LANES), v(n_seq, 24, LANES), v(3 * K, LANES), v(n_dp, 12, LANES),
            pltpu.SemaphoreType.DMA((2 * tiles + 1,)),
            pltpu.SemaphoreType.DMA((4,)),
            pltpu.SemaphoreType.DMA((tiles,)),
            pltpu.SemaphoreType.DMA((4,)),
        ],
        compiler_params=pltpu.CompilerParams(
            collective_id=0, has_side_effects=True, vmem_limit_bytes=40 * 2**20
        ),
        name="attend",
    )(tokens, cotangent, short_weights)


def last_kernel(entries, grads_ref, total_ref, squares_ref, out_ref, gw_ref, sem):
    pieces = sem.shape[0]
    rows = grads_ref.shape[1] // pieces
    copies = [
        pltpu.make_async_copy(
            grads_ref.at[0, pl.ds(r * rows, rows)], out_ref.at[0, pl.ds(r * rows, rows)], sem.at[r]
        )
        for r in range(pieces)
    ]
    for c in copies:
        c.start()
    mean_sq = jnp.full((8, LANES), jnp.sum(squares_ref[...]) / entries, F32)
    factor = jnp.minimum(1.0, 1.0 / jnp.sqrt(mean_sq + 1e-06))
    p = total_ref[0:8] * factor
    r = total_ref[8:12] * factor[:4]
    gw_ref[0] = p[:, :HEAD]
    gw_ref[1] = swap_halves(p)[:, :HEAD]
    gw_ref[2, 0:4] = r[:, :HEAD]
    gw_ref[2, 4:8] = swap_halves(r)[:, :HEAD]
    for c in copies:
        c.wait()


def last_call(grads, total, squares, entries):
    vmem = pl.BlockSpec(memory_space=pltpu.VMEM)
    return pl.pallas_call(
        functools.partial(last_kernel, entries),
        out_shape=(
            jax.ShapeDtypeStruct(grads.shape, F32),
            jax.ShapeDtypeStruct((3, K, HEAD), F32),
        ),
        in_specs=[vmem] * 3,
        out_specs=(pl.BlockSpec(memory_space=pltpu.HBM), vmem),
        scratch_shapes=[pltpu.SemaphoreType.DMA((8,))],
        compiler_params=pltpu.CompilerParams(vmem_limit_bytes=16 * 2**20),
        name="spread",
    )(grads, total, squares)


def solution(mesh):
    n_seq, n_dp = mesh.shape["seq"], mesh.shape["dp"]

    def per_device(tokens, cotangent, short_weights):
        grads, total, squares = main_call(tokens, cotangent, short_weights, n_seq, n_dp)
        return last_call(grads, total, squares, short_weights.size)

    return jax.shard_map(
        per_device,
        mesh=mesh,
        in_specs=(P("dp", "seq", None), P("dp", "seq", None), P()),
        out_specs=(P("dp", "seq", None), P(None, None, "seq")),
        check_vma=False,
    )
```

time: 134 us -> 58 us (0.43); the launches traced: 132 us -> 57.7 us
  waiting for transfers between devices: 55.6 us -> 0 us
  Pallas kernels: 0 us -> 53.7 us
  starting transfers between devices: 37 us -> 0 us
  local copies, waits for them, and re-layouts: 19.7 us -> 3.37 us
  matrix products: 11.3 us -> 0 us
  other arithmetic: 7.27 us -> 0 us
    all_to_all x5 -> x0, waiting for transfers between devices: 55.6 us -> none  [the longest x1 28.2 us: in_one_piece(): lax.all_to_all(both, axis, split_axis=split_dim, concat_axis=concat_dim,...]
    pallas_call x0 -> x2, Pallas kernels: none -> 53.7 us  [the longest x1 52.1 us: main_call(): pl.pallas_call(functools.partial(main_kernel, n_seq, n_dp), out_shape=(ja...]
    all_to_all x5 -> x0, starting transfers between devices: 37 us -> none  [the longest x2 16.4 us: from_everyone(): lax.all_to_all(jnp.broadcast_to(shard[None], (size, *shard.shape)), axis,...]
    dot_general x8 -> x0, matrix products: 11.3 us -> none  [the longest x1 2.2 us: per_device(): jnp.einsum('mbjc,bjic->mic', grad_summary, grouped, precision=hi)]
    slice x4 -> x0, local copies, waits for them, and re-layouts: 5.97 us -> none  [the longest x3 4.96 us: in_one_piece(): done.append(lax.slice_in_dim(result, at, at + a.shape[along], axis=along))]
    another operation x2 -> x0, local copies, waits for them, and re-layouts: 4.14 us -> none
    concatenate x1 -> x0, other arithmetic: 2.97 us -> none  [in_one_piece(): both = jnp.concatenate(arrays, axis=along)]
    reduce_sum x5 -> x0, other arithmetic: 2.8 us -> none  [the longest x1 1.33 us: per_device(): grad_o = jnp.sum(col_grad.reshape(batch, sums, K, width), axis=2)]
  transfers between devices with their start and end apart: 5 -> 0, of which waited for: 4 -> 0; matrix products, arithmetic and copies ran while one was open for 7% -> 0% of each run, Pallas kernels for 0% -> 0%
where the time goes in v1:
time: 58 us; the launch traced here: 57.7 us
  Pallas kernels  53.7 us (93%)
  local copies, waits for them, and re-layouts  3.37 us (6%)
  between operations  0.65 us (1%)
    pallas_call x1, Pallas kernels, main_call(): pl.pallas_call(functools.partial(main_kernel, n_seq, n_dp), out_shape=(ja...  52.1 us
    unnamed x6, local copies, waits for them, and re-layouts  3.37 us
    pallas_call x1, Pallas kernels, last_call(): pl.pallas_call(functools.partial(last_kernel, entries), out_shape=(jax.Sh...  1.63 us

profile of v1, /device:TPU:1, one launch (start us, length us, event | category | flops | bytes accessed | tf_op | source)
XLA Modules:
  0.0 57.7 jit_solution(17392622369807903467)
XLA Ops:
  0.6 0.0 copy-start
  0.6 1.2 %copy-done = f32[1,128,2048]{2,1,0:T(8,128)S(1)} copy-done((f32[1,128,2048]{2,1,0:T(8,128)S(1)}, f32[1,128,2048]{2,1,0:T(8,128)}, u32[]{:S(2)}) %copy-start) | copy-done | bytes 1048600
  1.9 0.0 copy-start.1
  1.9 1.2 %copy-done.1 = f32[1,128,2048]{2,1,0:T(8,128)S(1)} copy-done((f32[1,128,2048]{2,1,0:T(8,128)S(1)}, f32[1,128,2048]{2,1,0:T(8,128)}, u32[]{:S(2)}) %copy-start.1) | copy-done | bytes 1048600
  3.1 0.0 copy-start.2
  3.1 0.9 %copy-done.2 = f32[3,8,2048]{2,1,0:T(8,128)S(1)} copy-done((f32[3,8,2048]{2,1,0:T(8,128)S(1)}, f32[3,8,2048]{2,1,0:T(8,128)}, u32[]{:S(2)}) %copy-start.2) | copy-done | bytes 196632
  4.0 52.1 %attend.1 = (f32[1,128,2048]{2,1,0:T(8,128)S(1)}, f32[12,128]{1,0:T(8,128)S(1)}, f32[32,1,128]{2,1,0:T(1,128)S(1)}) custom-call(f32[1,128,2048]{2,1,0:T(8,128)S(1)} %copy-done, f32[1,128,2048]{2,1,0:T(8,128)S(1)} %copy-done.1, f32[3,8,2048]{2,1,0:T(8,128)S(1)} %copy-done.2), custom_call_target="tpu_custom_call" | custom-call | tf_op jit(solution)/shard_map/attend/pallas_call | solution.py:299
  56.1 1.6 %spread.1 = (f32[1,128,2048]{2,1,0:T(8,128)}, f32[3,8,64]{2,1,0:T(8,128)}) custom-call(f32[1,128,2048]{2,1,0:T(8,128)S(1)} %get-tuple-element.5.grads_ref, f32[12,128]{1,0:T(8,128)S(1)} %get-tuple-element.6.total_ref, f32[32,1,128]{2,1,0:T(1,128)S(1)} %get-tuple-element.7.squares_ref), custom_call_target="tpu_custom_call" | custom-call | tf_op jit(solution)/shard_map/spread/pallas_call | solution.py:353
Async XLA Ops:
  0.6 1.2 %copy-start = (f32[1,128,2048]{2,1,0:T(8,128)S(1)}, f32[1,128,2048]{2,1,0:T(8,128)}, u32[]{:S(2)}) copy-start(f32[1,128,2048]{2,1,0:T(8,128)} %tok_hbm.1) | copy-start | bytes 3145732
  1.9 1.2 %copy-start.1 = (f32[1,128,2048]{2,1,0:T(8,128)S(1)}, f32[1,128,2048]{2,1,0:T(8,128)}, u32[]{:S(2)}) copy-start(f32[1,128,2048]{2,1,0:T(8,128)} %cot_hbm.1) | copy-start | bytes 3145732
  3.1 0.9 %copy-start.2 = (f32[3,8,2048]{2,1,0:T(8,128)S(1)}, f32[3,8,2048]{2,1,0:T(8,128)}, u32[]{:S(2)}) copy-start(f32[3,8,2048]{2,1,0:T(8,128)} %w_hbm.1) | copy-start | bytes 589828

commit v2 on v1

--- a/solution.py
+++ b/solution.py
@@ -10,10 +10,13 @@
 HEAD = 64
 LANES = 128
 K = 8
+WIDE = 256
 GROUP = 16
 SCALE = HEAD ** (-0.5)
 LOG2E = 1.4426950408889634
 MESH = pl.DeviceIdType.MESH
+STEPS = sorted(((a, b) for a in range(4) for b in range(4)), key=lambda t: min(t[0], 4 - t[0]) + min(t[1], 4 - t[1]))
+FAR_FIRST = [(a, b, c) for a, b in STEPS[::-1] for c in range(2) if (a, b, c) != (0, 0, 0)]
 NT = (((1,), (1,)), ((), ()))
 NN = (((1,), (0,)), ((), ()))
 F32, BF16 = jnp.float32, jnp.bfloat16
@@ -57,7 +60,7 @@
     qs, ks, qc, os, vs, oc, kc, kt,
     acc_k, acc_v, acc_q,
     ret, back, rows, dp_all,
-    load_sem, send_sem, in_sem, recv_sem,
+    load_sem, send_sem, in_sem, recv_sem, relay,
 ):
     me = lax.axis_index("seq")
     plane = lax.axis_index("dp")
@@ -74,13 +77,12 @@
         pl.semaphore_signal(barrier, inc=1, device_id=(plane, other), device_id_type=MESH)
         return 0
 
-    def hello_dp(d, _):
-        other = lax.rem(plane + d, n_dp)
-        pl.semaphore_signal(barrier, inc=1, device_id=(other, me), device_id_type=MESH)
-        return 0
+    def tell_planes(sem, d):
+        for other in (lax.rem(plane + d, n_dp), lax.rem(plane + n_dp - d, n_dp)):
+            pl.semaphore_signal(sem, inc=1, device_id=(other, me), device_id_type=MESH)
 
     lax.fori_loop(1, n_seq, hello_seq, 0)
-    lax.fori_loop(1, n_dp, hello_dp, 0)
+    tell_planes(barrier, 1)
 
     def tile_loads(t):
         lanes = pl.ds(pl.multiple_of(t * LANES, LANES), LANES)
@@ -124,30 +126,29 @@
         for i in range(K):
             wb[K * m + i] = jnp.broadcast_to(mine[i : i + 1], (8, LANES))
 
-    pl.semaphore_wait(barrier, n_seq + n_dp - 2)
+    pl.semaphore_wait(barrier, n_seq + 1)
+    tell_planes(relay.at[0], 1)
 
     def to_seq(src_of, dst, s, sem_of):
-        def one(e, _):
-            k = e // 2
-            x, y = lax.rem(cx + k // 4, 4), lax.rem(cy + lax.rem(k, 4), 4)
-            other = (x * 4 + y) * 2 + lax.rem(core + lax.rem(e, 2), 2)
+        for a, b, c in FAR_FIRST:
+            dx, dy = a + core * (b - a), b + core * (a - b)
+            other = (((cx + dx) & 3) * 4 + ((cy + dy) & 3)) * 2 + (core ^ c)
             pltpu.make_async_remote_copy(
                 src_ref=src_of(other),
                 dst_ref=dst.at[me],
                 send_sem=send_sem.at[s],
-                recv_sem=sem_of(k),
+                recv_sem=sem_of(4 * dx + dy),
                 device_id=(plane, other),
                 device_id_type=MESH,
             ).start()
-            return 0
-
-        lax.fori_loop(1, n_seq, one, 0)
 
     def arrived(dst, sem):
         pltpu.make_async_copy(dst, dst, sem).wait()
 
     to_seq(lambda h: send.at[h], recv, 0, lambda k: in_sem.at[k])
     pltpu.make_async_copy(send.at[me], recv.at[me], in_sem.at[0]).start()
+    pl.semaphore_wait(relay.at[0], 2)
+    tell_planes(relay.at[1], 2)
 
     def query_role(x, side, cols, r0):
         for part, r in zip(both_halves(x), (r0, half + r0)):
@@ -167,8 +168,9 @@
             if keep is not None:
                 keep[at, :] = c
 
-    def take(k, _):
-        x, y = lax.rem(cx + 4 - k // 4, 4), lax.rem(cy + 4 - lax.rem(k, 4), 4)
+    def take(e, _):
+        k = e ^ 10
+        x, y = (cx - (k >> 2)) & 3, (cy - (k & 3)) & 3
         c = x * 4 + y
         block = recv.at[pl.ds(2 * c, 2)]
         arrived(block, in_sem.at[k])
@@ -187,11 +189,14 @@
         query_role(o, os, oc, r0)
         return 0
 
-    lax.fori_loop(0, tiles, take, 0)
+    lax.fori_loop(0, tiles // 2, take, 0)
+    pl.semaphore_wait(relay.at[1], 2)
+    tell_planes(relay.at[2], 4)
+    lax.fori_loop(tiles // 2, tiles, take, 0)
 
     kt[...] = kc[...].T.astype(BF16)
-    for b in range(2):
-        cols = slice(b * half, (b + 1) * half)
+    for at in range(0, sums, WIDE):
+        cols = slice(at, at + WIDE)
         s = dot(ks[...], qs[cols, :], NT)
         top = jnp.max(s, axis=0, keepdims=True)
         e = jnp.exp2((s - top) * (SCALE * LOG2E))
@@ -203,14 +208,15 @@
         g_high, g_low = (x.astype(BF16) for x in two_parts(gs))
         gv = dot(p_high, oc[cols, :], NN) + dot(p_low, oc[cols, :], NN)
         gk = dot(g_high, qc[cols, :], NN) + dot(g_low, qc[cols, :], NN)
-        if b == 0:
+        if at == 0:
             acc_v[...] = gv
             acc_k[...] = gk
         else:
             acc_v[...] += gv
             acc_k[...] += gk
         gq = dot(kt[...], g_high, NN) + dot(kt[...], g_low, NN)
-        acc_q[b * HEAD : (b + 1) * HEAD, :] = gq[:HEAD] + gq[HEAD:]
+        first = HEAD * (at // half)
+        acc_q[first : first + HEAD, at % half : at % half + WIDE] = gq[:HEAD] + gq[HEAD:]
 
     def packed(acc):
         x = acc[...]
@@ -242,6 +248,7 @@
     dp_all[plane, 0:8] = jnp.where(low, x[0:8], x[8:16])
     dp_all[plane, 8:12] = jnp.where(low[:4], x[16:20], x[20:24])
 
+    pl.semaphore_wait(relay.at[2], 2)
     for k in range(1, n_dp):
         d = n_dp // 2 + (k // 2 if k % 2 else -(k // 2))
         other = lax.rem(plane + d, n_dp)
@@ -317,12 +324,13 @@
             pltpu.SemaphoreType.DMA((4,)),
             pltpu.SemaphoreType.DMA((tiles,)),
             pltpu.SemaphoreType.DMA((4,)),
+            pltpu.SemaphoreType.REGULAR((3,)),
         ],
         compiler_params=pltpu.CompilerParams(
             collective_id=0, has_side_effects=True, vmem_limit_bytes=40 * 2**20
         ),
         name="attend",
-    )(tokens, cotangent, short_weights)
+    )(*(pltpu.with_memory_space_constraint(x, pltpu.HBM) for x in (tokens, cotangent, short_weights)))
 
 
 def last_kernel(entries, grads_ref, total_ref, squares_ref, out_ref, gw_ref, sem):

time: 58 us -> 49.8 us (0.86)
  Pallas kernels: 53.7 us -> 49.1 us
  local copies, waits for them, and re-layouts: 3.37 us -> 0 us
    pallas_call x1, Pallas kernels: 52.1 us -> 47.4 us  [main_call(): pl.pallas_call(functools.partial(main_kernel, n_seq, n_dp), out_shape=(ja...]
    unnamed x6 -> x0, local copies, waits for them, and re-layouts: 3.37 us -> none
where the time goes in v2:
time: 49.8 us; the launch traced here: 49.7 us
  Pallas kernels  49.1 us (99%)
  between operations  0.64 us (1%)
    pallas_call x1, Pallas kernels, main_call(): pl.pallas_call(functools.partial(main_kernel, n_seq, n_dp), out_shape=(ja...  47.4 us
    pallas_call x1, Pallas kernels, last_call(): pl.pallas_call(functools.partial(last_kernel, entries), out_shape=(jax.Sh...  1.63 us

profile of v2, /device:TPU:1, one launch (start us, length us, event | category | flops | bytes accessed | tf_op | source)
XLA Modules:
  0.0 49.7 jit_solution(12981128345481717597)
XLA Ops:
  0.6 47.4 %attend.1 = (f32[1,128,2048]{2,1,0:T(8,128)S(1)}, f32[12,128]{1,0:T(8,128)S(1)}, f32[32,1,128]{2,1,0:T(1,128)S(1)}) custom-call(f32[1,128,2048]{2,1,0:T(8,128)} %tok_hbm.1, f32[1,128,2048]{2,1,0:T(8,128)} %cot_hbm.1, f32[3,8,2048]{2,1,0:T(8,128)} %w_hbm.1), custom_call_target="tpu_custom_call" | custom-call | tf_op jit(solution)/shard_map/attend/pallas_call | solution.py:306
  48.1 1.6 %spread.1 = (f32[1,128,2048]{2,1,0:T(8,128)}, f32[3,8,64]{2,1,0:T(8,128)}) custom-call(f32[1,128,2048]{2,1,0:T(8,128)S(1)} %get-tuple-element.5.grads_ref, f32[12,128]{1,0:T(8,128)S(1)} %get-tuple-element.6.total_ref, f32[32,1,128]{2,1,0:T(1,128)S(1)} %get-tuple-element.7.squares_ref), custom_call_target="tpu_custom_call" | custom-call | tf_op jit(solution)/shard_map/spread/pallas_call | solution.py:361

commit v3 on v2

--- a/solution.py
+++ b/solution.py
@@ -10,6 +10,7 @@
 HEAD = 64
 LANES = 128
 K = 8
+TOGETHER = 2
 WIDE = 256
 GROUP = 16
 SCALE = HEAD ** (-0.5)
@@ -72,16 +73,18 @@
 
     barrier = pltpu.get_barrier_semaphore()
 
-    def hello_seq(d, _):
-        other = lax.rem(me + d, n_seq)
-        pl.semaphore_signal(barrier, inc=1, device_id=(plane, other), device_id_type=MESH)
-        return 0
+    partners = []
+    for a, b, c in FAR_FIRST:
+        dx, dy = a + core * (b - a), b + core * (a - b)
+        other = (((cx + dx) & 3) * 4 + ((cy + dy) & 3)) * 2 + (core ^ c)
+        partners.append((4 * dx + dy, other))
 
     def tell_planes(sem, d):
         for other in (lax.rem(plane + d, n_dp), lax.rem(plane + n_dp - d, n_dp)):
             pl.semaphore_signal(sem, inc=1, device_id=(other, me), device_id_type=MESH)
 
-    lax.fori_loop(1, n_seq, hello_seq, 0)
+    for _, other in partners:
+        pl.semaphore_signal(barrier, inc=1, device_id=(plane, other), device_id_type=MESH)
     tell_planes(barrier, 1)
 
     def tile_loads(t):
@@ -130,14 +133,12 @@
     tell_planes(relay.at[0], 1)
 
     def to_seq(src_of, dst, s, sem_of):
-        for a, b, c in FAR_FIRST:
-            dx, dy = a + core * (b - a), b + core * (a - b)
-            other = (((cx + dx) & 3) * 4 + ((cy + dy) & 3)) * 2 + (core ^ c)
+        for k, other in partners:
             pltpu.make_async_remote_copy(
                 src_ref=src_of(other),
                 dst_ref=dst.at[me],
                 send_sem=send_sem.at[s],
-                recv_sem=sem_of(4 * dx + dy),
+                recv_sem=sem_of(k),
                 device_id=(plane, other),
                 device_id_type=MESH,
             ).start()
@@ -149,6 +150,8 @@
     pltpu.make_async_copy(send.at[me], recv.at[me], in_sem.at[0]).start()
     pl.semaphore_wait(relay.at[0], 2)
     tell_planes(relay.at[1], 2)
+    pl.semaphore_wait(relay.at[1], 2)
+    tell_planes(relay.at[2], 4)
 
     def query_role(x, side, cols, r0):
         for part, r in zip(both_halves(x), (r0, half + r0)):
@@ -168,53 +171,56 @@
             if keep is not None:
                 keep[at, :] = c
 
+    def source(e):
+        k = e ^ 10
+        return k, ((cx - (k >> 2)) & 3) * 4 + ((cy - (k & 3)) & 3)
+
     def take(e, _):
-        k = e ^ 10
-        x, y = (cx - (k >> 2)) & 3, (cy - (k & 3)) & 3
-        c = x * 4 + y
-        block = recv.at[pl.ds(2 * c, 2)]
-        arrived(block, in_sem.at[k])
-        pooled = []
-        for m in range(3):
-            s = None
-            for i in range(K):
-                a = recv[pl.ds(2 * c, 2), 8 * i : 8 * i + 8, :] * wb[K * m + i]
-                s = a if s is None else s + a
-            pooled.append(s.reshape(GROUP, LANES))
-        o = recv[pl.ds(2 * c, 2), 8 * K : 8 * K + 8, :].reshape(GROUP, LANES)
-        r0 = c * GROUP
-        query_role(pooled[0], qs, qc, r0)
-        key_role(pooled[1], ks, r0, kc)
-        key_role(pooled[2], vs, r0)
-        query_role(o, os, oc, r0)
+        chips = []
+        for k, c in (source(TOGETHER * e + n) for n in range(TOGETHER)):
+            arrived(recv.at[pl.ds(2 * c, 2)], in_sem.at[k])
+            chips.append(c)
+        for c in chips:
+            pooled = []
+            for m in range(3):
+                s = None
+                for i in range(K):
+                    a = recv[pl.ds(2 * c, 2), 8 * i : 8 * i + 8, :] * wb[K * m + i]
+                    s = a if s is None else s + a
+                pooled.append(s.reshape(GROUP, LANES))
+            o = recv[pl.ds(2 * c, 2), 8 * K : 8 * K + 8, :].reshape(GROUP, LANES)
+            r0 = c * GROUP
+            query_role(pooled[0], qs, qc, r0)
+            key_role(pooled[1], ks, r0, kc)
+            key_role(pooled[2], vs, r0)
+            query_role(o, os, oc, r0)
         return 0
 
-    lax.fori_loop(0, tiles // 2, take, 0)
-    pl.semaphore_wait(relay.at[1], 2)
-    tell_planes(relay.at[2], 4)
-    lax.fori_loop(tiles // 2, tiles, take, 0)
+    lax.fori_loop(0, tiles // TOGETHER, take, 0)
 
     kt[...] = kc[...].T.astype(BF16)
     for at in range(0, sums, WIDE):
         cols = slice(at, at + WIDE)
         s = dot(ks[...], qs[cols, :], NT)
+        gp = dot(vs[...], os[cols, :], NT)
         top = jnp.max(s, axis=0, keepdims=True)
         e = jnp.exp2((s - top) * (SCALE * LOG2E))
-        p = e * (1.0 / jnp.sum(e, axis=0, keepdims=True))
-        gp = dot(vs[...], os[cols, :], NT)
-        delta = jnp.sum(p * gp, axis=0, keepdims=True)
+        r = 1.0 / jnp.sum(e, axis=0, keepdims=True)
+        delta = jnp.sum(e * gp, axis=0, keepdims=True) * r
+        p = e * r
         gs = p * (gp - delta)
         p_high, p_low = (x.astype(BF16) for x in two_parts(p))
         g_high, g_low = (x.astype(BF16) for x in two_parts(gs))
-        gv = dot(p_high, oc[cols, :], NN) + dot(p_low, oc[cols, :], NN)
-        gk = dot(g_high, qc[cols, :], NN) + dot(g_low, qc[cols, :], NN)
+        o, q, k = oc[cols, :], qc[cols, :], kt[...]
+        gv = dot(jnp.concatenate([p_high, p_low], 1), jnp.concatenate([o, o], 0), NN)
+        gk = dot(jnp.concatenate([g_high, g_low], 1), jnp.concatenate([q, q], 0), NN)
         if at == 0:
             acc_v[...] = gv
             acc_k[...] = gk
         else:
             acc_v[...] += gv
             acc_k[...] += gk
-        gq = dot(kt[...], g_high, NN) + dot(kt[...], g_low, NN)
+        gq = dot(jnp.concatenate([k, k], 1), jnp.concatenate([g_high, g_low], 0), NN)
         first = HEAD * (at // half)
         acc_q[first : first + HEAD, at % half : at % half + WIDE] = gq[:HEAD] + gq[HEAD:]
 
@@ -237,7 +243,7 @@
         return tuple(done)
 
     zero = jnp.zeros((8, LANES), F32)
-    acc = lax.fori_loop(0, n_seq, raw_step, (zero,) * (3 * K))
+    acc = lax.fori_loop(0, n_seq, raw_step, (zero,) * (3 * K), unroll=2)
     for i in range(K):
         for m in range(3):
             r = K * m + i
@@ -249,9 +255,8 @@
     dp_all[plane, 8:12] = jnp.where(low[:4], x[16:20], x[20:24])
 
     pl.semaphore_wait(relay.at[2], 2)
-    for k in range(1, n_dp):
-        d = n_dp // 2 + (k // 2 if k % 2 else -(k // 2))
-        other = lax.rem(plane + d, n_dp)
+    for k in range(n_dp - 1):
+        other = k + (k >= plane).astype(jnp.int32)
         pltpu.make_async_remote_copy(
             src_ref=dp_all.at[plane],
             dst_ref=dp_all.at[plane],

time: 49.8 us -> 49.2 us (0.988)
  Pallas kernels: 49.1 us -> 48.4 us
    pallas_call x1, Pallas kernels: 47.4 us -> 46.7 us  [main_call(): pl.pallas_call(functools.partial(main_kernel, n_seq, n_dp), out_shape=(ja...]
where the time goes in v3:
time: 49.2 us; the launch traced here: 49 us
  Pallas kernels  48.4 us (98%)
  between operations  0.64 us (1%)
    pallas_call x1, Pallas kernels, main_call(): pl.pallas_call(functools.partial(main_kernel, n_seq, n_dp), out_shape=(ja...  46.7 us
    pallas_call x1, Pallas kernels, last_call(): pl.pallas_call(functools.partial(last_kernel, entries), out_shape=(jax.Sh...  1.63 us

profile of v3, /device:TPU:1, one launch (start us, length us, event | category | flops | bytes accessed | tf_op | source)
XLA Modules:
  0.0 49.0 jit_solution(9206424811396696726)
XLA Ops:
  0.6 46.7 %attend.1 = (f32[1,128,2048]{2,1,0:T(8,128)S(1)}, f32[12,128]{1,0:T(8,128)S(1)}, f32[32,1,128]{2,1,0:T(1,128)S(1)}) custom-call(f32[1,128,2048]{2,1,0:T(8,128)} %tok_hbm.1, f32[1,128,2048]{2,1,0:T(8,128)} %cot_hbm.1, f32[3,8,2048]{2,1,0:T(8,128)} %w_hbm.1), custom_call_target="tpu_custom_call" | custom-call | tf_op jit(solution)/shard_map/attend/pallas_call | solution.py:311
  47.4 1.6 %spread.1 = (f32[1,128,2048]{2,1,0:T(8,128)}, f32[3,8,64]{2,1,0:T(8,128)}) custom-call(f32[1,128,2048]{2,1,0:T(8,128)S(1)} %get-tuple-element.5.grads_ref, f32[12,128]{1,0:T(8,128)S(1)} %get-tuple-element.6.total_ref, f32[32,1,128]{2,1,0:T(1,128)S(1)} %get-tuple-element.7.squares_ref), custom_call_target="tpu_custom_call" | custom-call | tf_op jit(solution)/shard_map/spread/pallas_call | solution.py:366

commit v4 on v3

--- a/solution.py
+++ b/solution.py
@@ -11,13 +11,13 @@
 LANES = 128
 K = 8
 TOGETHER = 2
-WIDE = 256
+WIDE = 512
 GROUP = 16
 SCALE = HEAD ** (-0.5)
 LOG2E = 1.4426950408889634
 MESH = pl.DeviceIdType.MESH
-STEPS = sorted(((a, b) for a in range(4) for b in range(4)), key=lambda t: min(t[0], 4 - t[0]) + min(t[1], 4 - t[1]))
-FAR_FIRST = [(a, b, c) for a, b in STEPS[::-1] for c in range(2) if (a, b, c) != (0, 0, 0)]
+STEPS = ((2, 2), (1, 2), (3, 2), (2, 1), (2, 3), (1, 1), (3, 3), (1, 3), (3, 1), (2, 0), (0, 2), (1, 0), (3, 0), (0, 1), (0, 3), (0, 0))
+FAR_FIRST = [(a, b, c) for a, b in STEPS for c in range(2) if (a, b, c) != (0, 0, 0)]
 NT = (((1,), (1,)), ((), ()))
 NN = (((1,), (0,)), ((), ()))
 F32, BF16 = jnp.float32, jnp.bfloat16
@@ -221,8 +221,9 @@
             acc_v[...] += gv
             acc_k[...] += gk
         gq = dot(jnp.concatenate([k, k], 1), jnp.concatenate([g_high, g_low], 0), NN)
-        first = HEAD * (at // half)
-        acc_q[first : first + HEAD, at % half : at % half + WIDE] = gq[:HEAD] + gq[HEAD:]
+        gq = gq[:HEAD] + gq[HEAD:]
+        acc_q[:HEAD] = gq[:, :half]
+        acc_q[HEAD:] = gq[:, half:]
 
     def packed(acc):
         x = acc[...]
@@ -243,7 +244,7 @@
         return tuple(done)
 
     zero = jnp.zeros((8, LANES), F32)
-    acc = lax.fori_loop(0, n_seq, raw_step, (zero,) * (3 * K), unroll=2)
+    acc = lax.fori_loop(0, n_seq, raw_step, (zero,) * (3 * K), unroll=4)
     for i in range(K):
         for m in range(3):
             r = K * m + i

time: 49.2 us -> 48.2 us (0.980)
  Pallas kernels: 48.4 us -> 47.4 us
    pallas_call x1, Pallas kernels: 46.7 us -> 45.8 us  [main_call(): pl.pallas_call(functools.partial(main_kernel, n_seq, n_dp), out_shape=(ja...]
where the time goes in v4:
time: 48.2 us; the launch traced here: 48 us
  Pallas kernels  47.4 us (98%)
  between operations  0.64 us (1%)
    pallas_call x1, Pallas kernels, main_call(): pl.pallas_call(functools.partial(main_kernel, n_seq, n_dp), out_shape=(ja...  45.8 us
    pallas_call x1, Pallas kernels, last_call(): pl.pallas_call(functools.partial(last_kernel, entries), out_shape=(jax.Sh...  1.63 us

profile of v4, /device:TPU:1, one launch (start us, length us, event | category | flops | bytes accessed | tf_op | source)
XLA Modules:
  0.0 48.0 jit_solution(12223026532391044903)
XLA Ops:
  0.6 45.8 %attend.1 = (f32[1,128,2048]{2,1,0:T(8,128)S(1)}, f32[12,128]{1,0:T(8,128)S(1)}, f32[32,1,128]{2,1,0:T(1,128)S(1)}) custom-call(f32[1,128,2048]{2,1,0:T(8,128)} %tok_hbm.1, f32[1,128,2048]{2,1,0:T(8,128)} %cot_hbm.1, f32[3,8,2048]{2,1,0:T(8,128)} %w_hbm.1), custom_call_target="tpu_custom_call" | custom-call | tf_op jit(solution)/shard_map/attend/pallas_call | solution.py:312
  46.4 1.6 %spread.1 = (f32[1,128,2048]{2,1,0:T(8,128)}, f32[3,8,64]{2,1,0:T(8,128)}) custom-call(f32[1,128,2048]{2,1,0:T(8,128)S(1)} %get-tuple-element.5.grads_ref, f32[12,128]{1,0:T(8,128)S(1)} %get-tuple-element.6.total_ref, f32[32,1,128]{2,1,0:T(1,128)S(1)} %get-tuple-element.7.squares_ref), custom_call_target="tpu_custom_call" | custom-call | tf_op jit(solution)/shard_map/spread/pallas_call | solution.py:367
